TPU v7x, 256 devices: a whole 4x4x8 slice. The times are simulated.
256 devices in a mesh: tm: 32 (over z, x_hi, core), grp: 8 (over y, x_lo).
Axes of the slice: x: 4 (x_hi: 2, x_lo: 2; x = x_hi * 2 + x_lo), y: 4, z: 8, core: 2. Of those that a mesh axis runs over, the one named last changes fastest.
Arguments:
- frames_in: bfloat16 [512, 128, 8, 256], P('tm', 'grp'), may hold values from -6 to 6
- span_frames: int32 [32], P('tm'), may hold values from 5 to 13, as said below
- w_spatial: bfloat16 [3, 3, 256, 256], replicated, may hold values from -0.125 to 0.125
- w_temporal: bfloat16 [3, 256, 256], replicated, may hold values from -0.21875 to 0.21875
- w_down: bfloat16 [2, 2, 256, 256], replicated, may hold values from -0.1875 to 0.1875
- cotangent: bfloat16 [512, 64, 4, 256], P('tm', 'grp'), may hold values from -6 to 6
Outputs:
- down_out: bfloat16 [512, 64, 4, 256], P('tm', 'grp')
- grad_x: bfloat16 [512, 128, 8, 256], P('tm', 'grp')
- grad_spatial: float32 [3, 3, 256, 256], replicated
- grad_temporal: float32 [3, 256, 256], replicated
- grad_down: float32 [2, 2, 256, 256], replicated
Inputs may be any that keep to these rules, and one draw needn't show every extreme that they name: `span_frames`: each entry is 1 + 4k for a whole k >= 1; some time block uses the largest count 16 - 3.
All inputs are finite; a program needn't handle non-finite values.
Results may differ from a plain program's by a relative error of at most 0.01.
Values may be sent and summed in bfloat16 or wider, within the bound.
A program may use at most 64 MiB of HBM per device.

v0:
```python
import jax
import jax.numpy as jnp
from jax import lax
from jax.sharding import PartitionSpec as P


def passed_along(value, axis, by):
    count = lax.axis_size(axis)
    pairs = [(i, i + by) for i in range(count) if 0 <= i + by < count]
    return lax.ppermute(value, axis, pairs)


def activate(values):
    scaled = values * lax.rsqrt(jnp.mean(values * values, axis=-1, keepdims=True) + 1e-06)
    return jax.nn.silu(scaled)


def conv_forward(padded, weights, height, width):
    total = None
    for row_off in range(3):
        for col_off in range(3):
            piece = padded[:, row_off : row_off + height, col_off : col_off + width]
            term = jnp.einsum(
                "fhwc,cd->fhwd",
                piece,
                weights[row_off, col_off],
                preferred_element_type=jnp.float32,
            )
            total = term if total is None else total + term
    return total


def conv_backward(padded, weights, height, width):
    total = None
    for row_off in range(3):
        for col_off in range(3):
            piece = padded[:, 2 - row_off : 2 - row_off + height, 2 - col_off : 2 - col_off + width]
            term = jnp.einsum(
                "fhwd,cd->fhwc",
                piece,
                weights[row_off, col_off],
                preferred_element_type=jnp.float32,
            )
            total = term if total is None else total + term
    return total


def spatial_grad(padded, grads, height, width):
    rows_out = []
    for row_off in range(3):
        cols_out = []
        for col_off in range(3):
            piece = padded[:, row_off : row_off + height, col_off : col_off + width]
            cols_out.append(
                jnp.einsum("fhwc,fhwd->cd", piece, grads, preferred_element_type=jnp.float32)
            )
        rows_out.append(jnp.stack(cols_out))
    return jnp.stack(rows_out)


def pad_both(values):
    return jnp.pad(values, ((0, 0), (1, 1), (1, 1), (0, 0)))


def body(frames_in, span_frames, w_spatial, w_temporal, w_down, cotangent):
    slots, band_rows, width_cells, channels = frames_in.shape
    count_here = span_frames[0]
    valid = (jnp.arange(slots, dtype=jnp.int32) < count_here).astype(jnp.float32)[
        :, None, None, None
    ]
    x_float = frames_in.astype(jnp.float32)
    activated, pullback = jax.vjp(activate, x_float)
    acts = (activated * valid).astype(jnp.bfloat16)
    members = lax.axis_size("grp")
    grouped = acts.reshape(members, slots // members, band_rows, width_cells, channels)
    frames_only = lax.all_to_all(grouped, "grp", split_axis=0, concat_axis=2, tiled=True)[0]
    padded = pad_both(frames_only)
    result = conv_forward(padded, w_spatial, frames_only.shape[1], width_cells).astype(jnp.bfloat16)
    spatial_frames = result[None]
    padded_frames = padded[None]
    acts_pad = padded_frames[0]
    spatial = lax.all_to_all(
        spatial_frames, "grp", split_axis=2, concat_axis=0, tiled=True
    ).reshape(slots, band_rows, width_cells, channels)
    edge_frames = lax.dynamic_slice_in_dim(spatial, count_here - 2, 2, 0)
    previous = passed_along(edge_frames, "tm", 1)
    extended = jnp.concatenate([previous, spatial], 0)
    temporal_sum = None
    for k in range(3):
        term = jnp.einsum(
            "fhwc,cd->fhwd",
            extended[k : k + slots],
            w_temporal[k],
            preferred_element_type=jnp.float32,
        )
        temporal_sum = term if temporal_sum is None else temporal_sum + term
    y_out = ((x_float + temporal_sum) * valid).astype(jnp.bfloat16)
    y_blocks = y_out.reshape(slots, band_rows // 2, 2, width_cells // 2, 2, channels)
    down_out = jnp.einsum(
        "fiajbc,abcd->fijd", y_blocks, w_down, preferred_element_type=jnp.float32
    ).astype(jnp.bfloat16)
    grad_pre = jnp.einsum(
        "fijd,abcd->fiajbc", cotangent, w_down, preferred_element_type=jnp.float32
    )
    grad_y = (grad_pre.reshape(slots, band_rows, width_cells, channels) * valid).astype(
        jnp.bfloat16
    )
    grad_down = jnp.einsum(
        "fiajbc,fijd->abcd", y_blocks, cotangent, preferred_element_type=jnp.float32
    )
    next_grads = passed_along(grad_y[:2], "tm", -1)
    padded_grads = jnp.concatenate(
        [grad_y, jnp.zeros((2, band_rows, width_cells, channels), jnp.bfloat16)], 0
    )
    anchor = count_here * 0
    placed = lax.dynamic_update_slice(
        padded_grads, next_grads, (count_here, anchor, anchor, anchor)
    )
    grad_sum = None
    for k in range(3):
        term = jnp.einsum(
            "fhwd,cd->fhwc",
            placed[2 - k : 2 - k + slots],
            w_temporal[k],
            preferred_element_type=jnp.float32,
        )
        grad_sum = term if grad_sum is None else grad_sum + term
    grad_s = (grad_sum * valid).astype(jnp.bfloat16)
    grad_temporal = jnp.stack(
        [
            jnp.einsum(
                "fhwc,fhwd->cd", extended[k : k + slots], grad_y, preferred_element_type=jnp.float32
            )
            for k in range(3)
        ]
    )
    grads_frames = lax.all_to_all(grad_s, "grp", split_axis=0, concat_axis=1, tiled=True)
    frame_rows = grads_frames.shape[1]
    grad_a_frames = conv_backward(pad_both(grads_frames), w_spatial, frame_rows, width_cells)
    grad_spatial = spatial_grad(acts_pad, grads_frames, frame_rows, width_cells)
    grad_a = lax.all_to_all(grad_a_frames, "grp", split_axis=1, concat_axis=0, tiled=True)
    grad_x = (grad_y.astype(jnp.float32) + valid * pullback(grad_a)[0]).astype(jnp.bfloat16)
    grad_spatial, grad_temporal, grad_down = lax.psum(
        (grad_spatial, grad_temporal, grad_down), ("tm", "grp")
    )
    return (down_out, grad_x, grad_spatial, grad_temporal, grad_down)


def solution(mesh):
    return jax.shard_map(
        body,
        mesh=mesh,
        in_specs=(P("tm", "grp", None, None), P("tm"), P(), P(), P(), P("tm", "grp", None, None)),
        out_specs=(P("tm", "grp", None, None), P("tm", "grp", None, None), P(), P(), P()),
        check_vma=False,
    )
```

profile of v0, /device:TPU:1, one launch (start us, length us, event | category | flops | bytes accessed | tf_op | source)
XLA Modules:
  0.0 448.4 jit_solution(11456905397642039977)
XLA Ops:
  8.2 2.4 multiply_convert_fusion
  10.6 2.9 copy.67
  13.6 2.7 reshape.49
  16.6 5.3 %collective-permute-start.1 = (bf16[2,16,8,256]{3,2,1,0:T(8,128)(2,1)S(1)}, bf16[2,16,8,256]{3,2,1,0:T(8,128)(2,1)S(1)}, u32[]{:S(2)}, u32[]{:S(2)}) collective-permute-start(bf16[2,16,8,256]{3,2,1,0:T(8,128)(2,1)S(1)} %slice.161), channel_id=1, source_target_pairs={{8,0},{16,8},{24,16},{32,24},{40,32},{48,40},{56,48},{64,56},{72,6... | collective-permute-start | bytes 393224 | tf_op jit(solution)/shard_map/ppermute | solution.py:10
  23.0 2.4 collective-permute-done.1
  26.1 1.8 fusion.66
  28.9 17.8 %all_to_all.66 = bf16[16,16,8,256]{3,2,1,0:T(8,128)(2,1)S(1)} all-to-all(bf16[16,16,8,256]{3,2,1,0:T(8,128)(2,1)S(1)} %multiply_convert_fusion.1), channel_id=1, replica_groups=mesh['tm'=32,'grp'=8] {'grp'}, dimensions={0} | all-to-all | bytes 2097152 | tf_op jit(solution)/shard_map/all_to_all | solution.py:137
  51.9 2.5 copy.69
  54.5 4.7 %all-to-all-start.3 = ((f32[2,128,8,256]{3,2,0,1:T(8,128)}), f32[2,128,8,256]{3,2,0,1:T(8,128)}, u32[]{:S(2)}, u32[]{:S(2)}) async-start(f32[2,128,8,256]{3,2,0,1:T(8,128)} %copy.69), calls=%async_computation.3 | async-start | bytes 4194304 | tf_op jit(solution)/shard_map/all_to_all | solution.py:141
  59.5 24.8 %all-to-all-done.3 = f32[2,128,8,256]{3,2,0,1:T(8,128)} async-done(((f32[2,128,8,256]{3,2,0,1:T(8,128)}), f32[2,128,8,256]{3,2,0,1:T(8,128)}, u32[]{:S(2)}, u32[]{:S(2)}) %all-to-all-start.3) | async-done | bytes 2097184 | tf_op jit(solution)/shard_map/all_to_all | solution.py:141
  84.3 1.8 copy.70
  88.7 2.1 fusion.12
  92.0 4.2 all-to-all-start
  97.4 14.4 %all-to-all-done = bf16[8,2,16,8,256]{4,2,3,1,0:T(8,128)(2,1)} async-done(((bf16[8,2,16,8,256]{4,2,3,1,0:T(8,128)(2,1)}), bf16[8,2,16,8,256]{4,2,3,1,0:T(8,128)(2,1)}, u32[]{:S(2)}, u32[]{:S(2)}) %all-to-all-start) | async-done | bytes 1048608 | tf_op jit(solution)/shard_map/all_to_all | solution.py:76
  111.8 1.3 copy.62
  113.2 1.4 fusion.29
  124.5 1.6 copy.63
  126.1 4.2 all-to-all-start.1
  132.6 1.6 pad_maximum_fusion
  134.2 11.7 %all-to-all-done.1 = bf16[1,2,128,8,256]{4,3,1,0,2:T(8,128)(2,1)} async-done(((bf16[1,2,128,8,256]{4,3,1,0,2:T(8,128)(2,1)}), bf16[1,2,128,8,256]{4,3,1,0,2:T(8,128)(2,1)}, u32[]{:S(2)}, u32[]{:S(2)}) %all-to-all-start.1) | async-done | bytes 1048608 | tf_op jit(solution)/shard_map/all_to_all | solution.py:82
  147.3 9.1 %collective-permute-start = (bf16[2,16,8,256]{3,2,1,0:T(8,128)(2,1)S(1)}, bf16[2,16,8,256]{3,2,1,0:T(8,128)(2,1)S(1)}, u32[]{:S(2)}, u32[]{:S(2)}) collective-permute-start(bf16[2,16,8,256]{3,2,1,0:T(8,128)(2,1)S(1)} %constant_dynamic-slice_fusion), channel_id=1, source_target_pairs={{0,8},{8,16},{16,24},{24,32},{32,40},{40,48},{48,56},{56,64},{64,7... | collective-permute-start | bytes 393224 | tf_op jit(solution)/shard_map/ppermute | solution.py:10
  160.8 3.8 convolution_bitcast_fusion.1
  169.4 266.9 %all-reduce.6.cloned.1.call-done = (f32[3,3,256,256]{3,2,1,0:T(8,128)}, f32[3,256,256]{2,1,0:T(8,128)}, f32[2,2,256,256]{3,2,1,0:T(8,128)}) async-done(((f32[3,3,256,256]{3,2,1,0:T(8,128)}, f32[3,256,256]{2,1,0:T(8,128)}, f32[2,2,256,256]{3,2,1,0:T(8,128)}), (f32[3,3,256,256]{3,2,1,0:T(8,128)}, f32[3,256,256]{2,1,0:T(8,128)}, f32[2,2,256,256]{3,2,1,0:T(8,128)})) %all-reduce.6.cloned.1.call-update) | async-done | bytes 4194320 | tf_op jit(solution)/shard_map/psum | solution.py:143
  436.3 3.4 copy.145
  (102 shorter events, 38.2 us)
Async XLA Ops:
  7.2 1.1 copy-start
  16.3 6.8 %copy-start.3 = (f32[16,16,8,256]{3,2,1,0:T(8,128)}, f32[16,16,8,256]{3,2,1,0:T(8,128)S(1)}, u32[]{:S(2)}) copy-start(f32[16,16,8,256]{3,2,1,0:T(8,128)S(1)} %reshape.49) | copy-start | bytes 6291460
  16.6 5.3 %copy-start.6 = (bf16[16,16,8,256]{3,2,1,0:T(8,128)(2,1)}, bf16[16,16,8,256]{3,2,1,0:T(8,128)(2,1)S(1)}, u32[]{:S(2)}) copy-start(bf16[16,16,8,256]{3,2,1,0:T(8,128)(2,1)S(1)} %multiply_convert_fusion.2) | copy-start | bytes 3145732
  16.6 9.5 %copy-start.11 = (bf16[3,256,256]{2,1,0:T(8,128)(2,1)S(1)}, bf16[3,256,256]{2,1,0:T(8,128)(2,1)}, u32[]{:S(2)}) copy-start(bf16[3,256,256]{2,1,0:T(8,128)(2,1)} %param.9) | copy-start | bytes 1179652
  16.6 8.8 %collective-permute-start.1 = (bf16[2,16,8,256]{3,2,1,0:T(8,128)(2,1)S(1)}, bf16[2,16,8,256]{3,2,1,0:T(8,128)(2,1)S(1)}, u32[]{:S(2)}, u32[]{:S(2)}) collective-permute-start(bf16[2,16,8,256]{3,2,1,0:T(8,128)(2,1)S(1)} %slice.161), channel_id=1, source_target_pairs={{8,0},{16,8},{24,16},{32,24},{40,32},{48,40},{56,48},{64,56},{72,6... | collective-permute-start | bytes 393224 | tf_op jit(solution)/shard_map/ppermute | solution.py:10
  26.1 1.8 copy-start.5
  28.9 18.1 %copy-start.8 = (bf16[3,3,256,256]{3,2,1,0:T(8,128)(2,1)S(1)}, bf16[3,3,256,256]{3,2,1,0:T(8,128)(2,1)}, u32[]{:S(2)}) copy-start(bf16[3,3,256,256]{3,2,1,0:T(8,128)(2,1)} %param.8) | copy-start | bytes 3538948
  54.5 4.7 %copy-start.1 = (bf16[16,16,8,256]{3,2,1,0:T(8,128)(2,1)S(1)}, bf16[16,16,8,256]{3,2,1,0:T(8,128)(2,1)}, u32[]{:S(2)}) copy-start(bf16[16,16,8,256]{3,2,1,0:T(8,128)(2,1)} %param.6) | copy-start | bytes 3145732
  54.5 29.9 %all-to-all-start.3 = ((f32[2,128,8,256]{3,2,0,1:T(8,128)}), f32[2,128,8,256]{3,2,0,1:T(8,128)}, u32[]{:S(2)}, u32[]{:S(2)}) async-start(f32[2,128,8,256]{3,2,0,1:T(8,128)} %copy.69), calls=%async_computation.3 | async-start | bytes 4194304 | tf_op jit(solution)/shard_map/all_to_all | solution.py:141
  87.1 1.6 copy-start.4
  90.8 5.5 %copy-start.10 = (bf16[16,8,2,4,2,256]{5,0,3,1,4,2:T(8,128)(2,1)S(1)}, bf16[16,8,2,4,2,256]{5,0,3,1,4,2:T(8,128)(2,1)}, u32[]{:S(2)}) copy-start(bf16[16,8,2,4,2,256]{5,0,3,1,4,2:T(8,128)(2,1)} %get-tuple-element.25) | copy-start | bytes 3145732
  92.0 19.8 %all-to-all-start = ((bf16[8,2,16,8,256]{4,2,3,1,0:T(8,128)(2,1)}), bf16[8,2,16,8,256]{4,2,3,1,0:T(8,128)(2,1)}, u32[]{:S(2)}, u32[]{:S(2)}) async-start(bf16[8,2,16,8,256]{4,2,3,1,0:T(8,128)(2,1)} %copy.61), calls=%async_computation | async-start | bytes 2097152 | tf_op jit(solution)/shard_map/all_to_all | solution.py:76
  113.2 1.5 copy-start.9
  126.1 19.8 %all-to-all-start.1 = ((bf16[1,2,128,8,256]{4,3,1,0,2:T(8,128)(2,1)}), bf16[1,2,128,8,256]{4,3,1,0,2:T(8,128)(2,1)}, u32[]{:S(2)}, u32[]{:S(2)}) async-start(bf16[1,2,128,8,256]{4,3,1,0,2:T(8,128)(2,1)} %copy.63), calls=%async_computation.1 | async-start | bytes 2097152 | tf_op jit(solution)/shard_map/all_to_all | solution.py:82
  130.3 306.0 %all-reduce.6.cloned.1.call-start = ((), (), s32[]{:S(2)}) async-start(), calls=%async_computation.4 | async-start | bytes 8388608 | tf_op jit(solution)/shard_map/psum | solution.py:143
  130.4 1.0 copy-start.18
  134.2 22.2 %copy-start.14 = (bf16[16,8,2,4,2,256]{5,0,4,3,2,1:T(8,128)(2,1)S(1)}, bf16[16,8,2,4,2,256]{5,0,4,3,2,1:T(8,128)(2,1)}, u32[]{:S(2)}) copy-start(bf16[16,8,2,4,2,256]{5,0,4,3,2,1:T(8,128)(2,1)} %copy.80) | copy-start | bytes 3145732
  147.3 10.8 %collective-permute-start = (bf16[2,16,8,256]{3,2,1,0:T(8,128)(2,1)S(1)}, bf16[2,16,8,256]{3,2,1,0:T(8,128)(2,1)S(1)}, u32[]{:S(2)}, u32[]{:S(2)}) collective-permute-start(bf16[2,16,8,256]{3,2,1,0:T(8,128)(2,1)S(1)} %constant_dynamic-slice_fusion), channel_id=1, source_target_pairs={{0,8},{8,16},{16,24},{24,32},{32,40},{40,48},{48,56},{56,64},{64,7... | collective-permute-start | bytes 393224 | tf_op jit(solution)/shard_map/ppermute | solution.py:10
  157.7 1.2 copy-start.2
  159.6 1.2 copy-start.20
  160.8 3.8 copy-start.7
  166.6 1.2 copy-start.16
  436.3 3.4 copy-start.19
  436.3 4.2 copy-start.15
  (3 other events, 3.0 us)
Sparse Core Ops, SparseCore 0:
  166.8 269.4 all-reduce.5
where the time goes:
time: 450 us; the launch traced here: 448 us
  waiting for transfers between devices  321 us (71%)
  matrix products  30.7 us (7%)
  local copies, waits for them, and re-layouts  29.6 us (7%)
  starting transfers between devices  27.6 us (6%)
  blocking collectives  17.8 us (4%)
  between operations  15.2 us (3%)
  other arithmetic  6.78 us (2%)
    psum x1, waiting for transfers between devices, body(): lax.psum((grad_spatial, grad_temporal, grad_down), ('tm', 'grp'))  267 us
    all_to_all x1, waiting for transfers between devices, body(): lax.all_to_all(grad_a_frames, 'grp', split_axis=1, concat_axis=0, tiled=T...  24.8 us
    all_to_all x1, blocking collectives, body(): lax.all_to_all(grad_s, 'grp', split_axis=0, concat_axis=1, tiled=True)  17.8 us
    all_to_all x1, waiting for transfers between devices, body(): lax.all_to_all(grouped, 'grp', split_axis=0, concat_axis=2, tiled=True)[0]  14.4 us
    ppermute x2, starting transfers between devices, passed_along(): return lax.ppermute(value, axis, pairs)  14.4 us
    all_to_all x1, waiting for transfers between devices, body(): lax.all_to_all(spatial_frames, 'grp', split_axis=2, concat_axis=0, tiled=...  11.7 us
    unnamed x46, local copies, waits for them, and re-layouts  9.73 us
  transfers between devices with their start and end apart: 6, of which 6 were waited for; matrix products, arithmetic and copies ran while one was open for 2% of the time, Pallas kernels for 0%

commit v1 on v0

v1 whole, which is shorter than its diff:
```python
import functools

import jax
import jax.numpy as jnp
from jax import lax
from jax.experimental import pallas as pl
from jax.experimental.pallas import tpu as pltpu
from jax.sharding import PartitionSpec as P

MESH = pl.DeviceIdType.MESH
BF = jnp.bfloat16
F32 = jnp.float32
NT = (((1,), (1,)), ((), ()))
TN = (((0,), (0,)), ((), ()))


def mm(a, b):
    return jnp.dot(a, b, preferred_element_type=F32)


def mm_nt(a, b):
    return lax.dot_general(a, b, NT, preferred_element_type=F32)


def mm_tn(a, b):
    return lax.dot_general(a, b, TN, preferred_element_type=F32)


def onehot(cond):
    return jnp.where(cond, 1.0, 0.0).astype(BF)


def iotas(rows, cols):
    shape = (rows, cols)
    return lax.broadcasted_iota(jnp.int32, shape, 0), lax.broadcasted_iota(jnp.int32, shape, 1)


def kernel(
    n_tm,
    n_grp,
    span,
    x_hbm,
    cot_hbm,
    wsp_hbm,
    wt_hbm,
    wd_hbm,
    down_ref,
    gx_ref,
    gsp_ref,
    gt_ref,
    gd_ref,
    xv,
    cv,
    wsp,
    wt,
    wd,
    perm,
    cown,
    cext,
    gy,
    gyo,
    gs,
    xt,
    acts,
    acts_t,
    edge_rows,
    s_edge,
    s_next,
    r_acts,
    r_cot,
    r_edge,
    r_next,
    sp,
    y4,
    part,
    r_core,
    sum1,
    r_one,
    sum2,
    r_two,
    sum3,
    r_z,
    full,
    in_sem,
    h_send,
    h_recv,
    a_send,
    a_recv,
):
    t = lax.axis_index("tm")
    g = lax.axis_index("grp")
    core = lax.rem(t, 2)
    x = lax.rem(lax.div(t, 2), 2) * 2 + lax.rem(g, 2)
    y = lax.div(g, 2)
    z = lax.div(t, 4)
    count = span[0]

    def device(px, py, pz, pc):
        return (pz * 4 + lax.div(px, 2) * 2 + pc, py * 2 + lax.rem(px, 2))

    def x_peer(d):
        px = lax.rem(x + d, 4)
        return px, device(px, y, z, core)

    def y_peer(d):
        py = lax.rem(y + d, 4)
        return py, device(x, py, z, core)

    def z_peer(d):
        pz = lax.rem(z + d, 8)
        return pz, device(x, y, pz, core)

    sibling = device(x, y, z, 1 - core)
    t_next, t_prev = lax.rem(t + 1, n_tm), lax.rem(t + n_tm - 1, n_tm)
    g_next, g_prev = lax.rem(g + 1, n_grp), lax.rem(g + n_grp - 1, n_grp)

    loads = [
        pltpu.make_async_copy(src, dst, in_sem.at[i])
        for i, (src, dst) in enumerate(
            ((cot_hbm, cv), (x_hbm, xv), (wd_hbm, wd), (wt_hbm, wt), (wsp_hbm, wsp))
        )
    ]
    for load in loads:
        load.start()

    partners = [(t, g_next), (t, g_prev), (t_next, g), (t_prev, g)]
    partners += [(t_next, g_next), (t_next, g_prev), (t_prev, g_next), (t_prev, g_prev)]
    partners += [sibling]
    partners += [x_peer(d)[1] for d in (1, 2, 3)]
    partners += [y_peer(d)[1] for d in (1, 2, 3)]
    partners += [z_peer(d)[1] for d in range(1, 8)]
    barrier = pltpu.get_barrier_semaphore()
    for partner in partners:
        pl.semaphore_signal(barrier, inc=1, device_id=partner, device_id_type=MESH)

    r, q = iotas(256, 256)
    perm[...] = onehot((lax.rem(r, 16) == lax.div(q, 16)) & (lax.div(r, 16) == lax.rem(q, 16)))
    slot = lax.rem(lax.broadcasted_iota(jnp.int32, (256, 256), 0), 16)
    valid = slot < count

    zeros16 = jnp.zeros((18, 16, 256), BF)
    for buffer in (acts, gs):
        buffer[:, 0:16, :] = zeros16
        buffer[:, 144:160, :] = zeros16

    loads[0].wait()
    r, q = iotas(64, 256)
    pick_next = onehot((lax.div(r, 4) == lax.div(q, 16)) & (lax.rem(r, 4) == lax.rem(q, 16)))
    for b in range(2):
        block = mm(perm[...], cv[:, 16 * b : 16 * b + 16, :].reshape(256, 256))
        block = jnp.where(valid, block, 0.0).astype(BF)
        cown[4 * b : 4 * b + 4] = block.reshape(4, 64, 256)
        s_next[4 * b : 4 * b + 4] = mm(pick_next, block).astype(BF).reshape(4, 16, 256)

    def halo(index, src, dst, to):
        return pltpu.make_async_remote_copy(
            src_ref=src,
            dst_ref=dst,
            send_sem=h_send.at[index],
            recv_sem=h_recv.at[index],
            device_id=to,
            device_id_type=MESH,
        )

    cot_halos = [
        halo(0, cown.at[7], r_cot.at[0], (t, g_next)),
        halo(1, cown.at[0], r_cot.at[1], (t, g_prev)),
        halo(2, s_next, r_next.at[pl.ds(1, 8)], (t_prev, g)),
        halo(3, s_next.at[7], r_next.at[0], (t_prev, g_next)),
        halo(4, s_next.at[0], r_next.at[9], (t_prev, g_prev)),
    ]
    act_halos = [
        halo(5, edge_rows.at[1], r_acts.at[0], (t, g_next)),
        halo(6, edge_rows.at[0], r_acts.at[1], (t, g_prev)),
    ]
    edge_halos = [
        halo(7, s_edge, r_edge.at[pl.ds(1, 16)], (t_next, g)),
        halo(8, s_edge.at[15], r_edge.at[0], (t_next, g_next)),
        halo(9, s_edge.at[0], r_edge.at[17], (t_next, g_prev)),
    ]
    pl.semaphore_wait(barrier, len(partners))
    for copy in cot_halos:
        copy.start()

    loads[1].wait()
    r, q = iotas(32, 256)
    pick_edge = onehot(
        (lax.div(r, 2) == lax.div(q, 16)) & (lax.rem(q, 16) == count - 2 + lax.rem(r, 2))
    )

    def activate(pair):
        rows = pl.ds(pl.multiple_of(16 * pair, 16), 16)
        v = mm(perm[...], xv[:, rows, :].reshape(256, 256))
        xt[pl.ds(2 * pair, 2)] = v.astype(BF).reshape(2, 128, 256)
        u = v * lax.rsqrt(jnp.mean(v * v, axis=-1, keepdims=True) + 1e-06)
        a = jnp.where(valid, u / (1.0 + jnp.exp(-u)), 0.0).astype(BF)
        acts[pl.ds(2 * pair + 1, 2), 16:144, :] = a.reshape(2, 128, 256)
        s_edge[pl.ds(2 * pair, 2)] = mm(pick_edge, a).astype(BF).reshape(2, 16, 256)
        return a

    edge_rows[0] = activate(0)[:128]
    edge_rows[1] = activate(7)[128:]
    for copy in act_halos:
        copy.start()

    @pl.loop(1, 7)
    def _(pair):
        activate(pair)

    for copy in edge_halos:
        copy.start()

    r, q = iotas(256, 256)
    eye = onehot(r == q)
    for pair in range(8):
        a = acts[2 * pair + 1 : 2 * pair + 3, 16:144, :].reshape(256, 256)
        acts_t[:, 256 * pair : 256 * pair + 256] = mm_nt(eye, a).astype(BF)

    for copy in cot_halos:
        copy.wait()
    loads[2].wait()
    r, q = iotas(256, 64)
    put_next = onehot(
        (lax.div(r, 16) == lax.div(q, 4))
        & (lax.rem(r, 16) == count + lax.rem(q, 4))
        & (lax.rem(q, 4) < 2)
        & (t < n_tm - 1)
    )
    for b in range(2):
        block = cown[4 * b : 4 * b + 4].reshape(256, 256).astype(F32)
        block += mm(put_next, r_next[4 * b + 1 : 4 * b + 5].reshape(64, 256))
        cext[4 * b + 1 : 4 * b + 5] = block.astype(BF).reshape(4, 64, 256)
    for side, row, inside in ((0, 0, g > 0), (1, 9, g < n_grp - 1)):
        block = r_cot[side].astype(F32) + mm(put_next[:64, :16], r_next[row])
        cext[row] = jnp.where(inside, block, 0.0).astype(BF)
    for i in range(2):
        for j in range(2):
            piece = mm_nt(cext[...].reshape(640, 256), wd[pl.ds((2 * i + j) * 256, 256), :])
            piece = piece.astype(BF).reshape(10, 4, 16, 256)
            for row in range(10):
                gy[2 * row + i, :, j] = piece[row]

    loads[3].wait()
    r, q = iotas(256, 256)
    same = lax.div(r, 16) == lax.div(q, 16)
    r, q = lax.rem(r, 16), lax.rem(q, 16)
    up1, up2 = onehot(same & (q == r + 1)), onehot(same & (q == r + 2))
    wt_back = jnp.concatenate([wt[512:768], wt[256:512], wt[0:256]], axis=1)

    @pl.loop(0, 9)
    def _(k):
        now = gy[pl.ds(2 * k + 1, 2)].reshape(256, 256)
        ext = jnp.concatenate([now, mm(up1, now).astype(BF), mm(up2, now).astype(BF)], axis=1)
        res = jnp.where(valid, mm_nt(ext, wt_back), 0.0).astype(BF)
        gs[pl.ds(2 * k, 2), 16:144, :] = res.reshape(2, 128, 256)

    @pl.loop(0, 8)
    def _(k):
        now = gy[pl.ds(2 * k + 2, 2)].reshape(256, 256).astype(F32)
        gyo[pl.ds(2 * k, 2)] = jnp.where(valid, now, 0.0).astype(BF).reshape(2, 128, 256)

    def keep(block, value):
        value = value.astype(BF)
        part[block // 8, 0, block % 8] = value[:, :128]
        part[block // 8, 1, block % 8] = value[:, 128:]

    for i in range(3):
        for j in range(3):
            piece = gs[2 - i : 18 - i, 16 * (2 - j) : 16 * (2 - j) + 128, :].reshape(2048, 256)
            keep(3 * i + j, mm(acts_t[...], piece))

    def reduction(n):
        def copy(index, src, dst, to):
            return pltpu.make_async_remote_copy(
                src_ref=src,
                dst_ref=dst,
                send_sem=a_send.at[n, index],
                recv_sem=a_recv.at[n, index],
                device_id=to,
                device_id_type=MESH,
            )

        state = {}

        def begin(copies):
            for c in copies:
                c.start()
            state["now"] = copies

        def finish():
            for c in state["now"]:
                c.wait()

        def s0():
            begin([copy(0, part.at[n, 1 - core], r_core.at[n], sibling)])

        def s1():
            finish()

            @pl.loop(0, 8)
            def _(b):
                total = part[n, core, b].astype(F32) + r_core[n, b].astype(F32)
                sum1[n, b] = total.astype(BF)

            copies = []
            for d in (1, 2, 3):
                px, to = x_peer(d)
                copies.append(copy(d, sum1.at[n, px], r_one.at[n, 0, d - 1], to))
                py, to = y_peer(d)
                copies.append(copy(3 + d, sum1.at[n, 4 + py], r_one.at[n, 1, d - 1], to))
            begin(copies)

        def s2():
            finish()
            for k, own in ((0, x), (1, 4 + y)):
                total = sum1[n, own].astype(F32)
                for d in range(3):
                    total += r_one[n, k, d].astype(F32)
                sum2[n, k] = total.astype(BF).reshape(4, 64, 128)
            copies = []
            for d in (1, 2, 3):
                py, to = y_peer(d)
                copies.append(copy(6 + d, sum2.at[n, 0, py], r_two.at[n, 0, d - 1], to))
                px, to = x_peer(d)
                copies.append(copy(9 + d, sum2.at[n, 1, px], r_two.at[n, 1, d - 1], to))
            begin(copies)

        def s3():
            finish()
            for k, own in ((0, y), (1, x)):
                total = sum2[n, k, own].astype(F32)
                for d in range(3):
                    total += r_two[n, k, d].astype(F32)
                sum3[n, 4 * k : 4 * k + 4] = total.astype(BF).reshape(4, 16, 128)
            copies = []
            for d in range(1, 8):
                pz, to = z_peer(d)
                copies.append(copy(12 + d, sum3.at[n, pz], r_z.at[n, d - 1], to))
            begin(copies)

        k = lax.div(z, 4)
        first, second = x * (1 - k) + y * k, y * (1 - k) + x * k

        def s4():
            finish()
            total = sum3[n, z].astype(F32)
            for d in range(7):
                total += r_z[n, d].astype(F32)
            full[n, core, k, first, second, lax.rem(z, 4)] = total.astype(BF)
            mine = full.at[n, core, k, first, second, lax.rem(z, 4)]
            begin([copy(19 + d, mine, mine, z_peer(d)[1]) for d in range(1, 8)])

        def s5():
            finish()
            one, two = full.at[n, core, 0, x, y], full.at[n, core, 1, y, x]
            copies = []
            for d in (1, 2, 3):
                copies.append(copy(26 + d, one, one, y_peer(d)[1]))
                copies.append(copy(29 + d, two, two, x_peer(d)[1]))
            begin(copies)

        def s6():
            finish()
            one, two = full.at[n, core, 0, x], full.at[n, core, 1, y]
            copies = []
            for d in (1, 2, 3):
                copies.append(copy(32 + d, one, one, x_peer(d)[1]))
                copies.append(copy(35 + d, two, two, y_peer(d)[1]))
            begin(copies)

        def s7():
            finish()
            begin([copy(39, full.at[n, core], full.at[n, core], sibling)])

        return [s0, s1, s2, s3, s4, s5, s6, s7, finish]

    red_a, red_b = reduction(0), reduction(1)
    red_a[0]()

    for copy in act_halos:
        copy.wait()
    for copy in edge_halos:
        copy.wait()
    r, q = iotas(256, 32)
    put_edge = onehot(
        (lax.div(r, 16) == lax.div(q, 2)) & (lax.rem(r, 16) == 14 + lax.rem(q, 2)) & (t > 0)
    )
    for k in range(8):
        block = acts[2 * k + 1 : 2 * k + 3, 16:144, :].reshape(256, 256).astype(F32)
        block += mm(put_edge, r_edge[2 * k + 1 : 2 * k + 3].reshape(32, 256))
        acts[2 * k + 1 : 2 * k + 3, 16:144, :] = block.astype(BF).reshape(2, 128, 256)
    for side, row, inside in ((0, 0, g > 0), (1, 17, g < n_grp - 1)):
        block = r_acts[side].astype(F32) + mm(put_edge[:128, :16], r_edge[row])
        acts[row, 16:144, :] = jnp.where(inside, block, 0.0).astype(BF)
    red_a[1]()

    loads[4].wait()
    r, q = iotas(256, 256)
    same = lax.div(r, 16) == lax.div(q, 16)
    r, q = lax.rem(r, 16), lax.rem(q, 16)
    back1 = onehot(same & (q == lax.rem(r + 15, 16)))
    back2 = onehot(same & (q == lax.rem(r + 14, 16)))

    def taps(buffer, start, flip):
        pieces = []
        for i in range(3):
            for j in range(3):
                a, b = (2 - i, 2 - j) if flip else (i, j)
                piece = buffer[pl.ds(start + a, 4), 16 * b : 16 * b + 128, :]
                pieces.append(piece.reshape(512, 256))
        return jnp.concatenate(pieces, axis=1)

    @pl.loop(0, 4)
    def _(k):
        res = mm(taps(acts, 4 * k, False), wsp[...]).astype(BF)
        rows = pl.ds(pl.multiple_of(512 * k, 512), 512)
        sp[2, rows, :] = res
        for half in range(2):
            rows = pl.ds(pl.multiple_of(512 * k + 256 * half, 256), 256)
            now = res[256 * half : 256 * half + 256]
            sp[1, rows, :] = mm(back1, now).astype(BF)
            sp[0, rows, :] = mm(back2, now).astype(BF)

    red_a[2]()

    slot5 = lax.rem(lax.broadcasted_iota(jnp.int32, (512, 256), 0), 16)
    valid5 = slot5 < count

    @pl.loop(0, 4)
    def _(k):
        rows = pl.ds(pl.multiple_of(512 * k, 512), 512)
        ext = jnp.concatenate([sp[0, rows, :], sp[1, rows, :], sp[2, rows, :]], axis=1)
        total = mm(ext, wt[...]) + xt[pl.ds(4 * k, 4)].reshape(512, 256).astype(F32)
        total = jnp.where(valid5, total, 0.0).astype(BF).reshape(2, 2, 4, 2, 16, 256)
        for i in range(2):
            for j in range(2):
                y4[2 * i + j, pl.ds(2 * k, 2)] = total[:, i, :, j].reshape(2, 64, 256)

    red_a[3]()
    for k in range(3):
        keep(9 + k, mm_tn(sp[k], gyo[...].reshape(2048, 256)))
    for k in range(4):
        keep(12 + k, mm_tn(y4[k].reshape(512, 256), cown[...].reshape(512, 256)))
    red_b[0]()
    red_a[4]()
    ext = jnp.concatenate([y4[k].reshape(512, 256) for k in range(4)], axis=1)
    res = mm(ext, wd[...]).astype(BF)
    for b in range(2):
        block = mm(perm[...], res[256 * b : 256 * b + 256]).astype(BF)
        down_ref[:, 16 * b : 16 * b + 16, :] = block.reshape(16, 16, 256)
    red_b[1]()
    red_a[5]()

    wsp_back = jnp.concatenate([wsp[256 * k : 256 * k + 256] for k in range(9)], axis=1)

    def finish_rows(k):
        ga = mm_nt(taps(gs, 4 * k, True), wsp_back)
        v = xt[pl.ds(4 * k, 4)].reshape(512, 256).astype(F32)
        inv = lax.rsqrt(jnp.mean(v * v, axis=-1, keepdims=True) + 1e-06)
        u = v * inv
        s = 1.0 / (1.0 + jnp.exp(-u))
        gu = ga * (s * (1.0 + u * (1.0 - s)))
        gv = inv * (gu - u * jnp.mean(gu * u, axis=-1, keepdims=True))
        res = gv + gyo[pl.ds(4 * k, 4)].reshape(512, 256).astype(F32)
        res = jnp.where(valid5, res, 0.0).astype(BF)
        for half in range(2):
            block = mm(perm[...], res[256 * half : 256 * half + 256]).astype(BF)
            rows = pl.ds(pl.multiple_of(32 * k + 16 * half, 16), 16)
            gx_ref[:, rows, :] = block.reshape(16, 16, 256)

    pl.loop(0, 2)(finish_rows)
    red_b[2]()
    red_a[6]()
    pl.loop(2, 4)(finish_rows)
    red_b[3]()
    red_a[7]()
    for step in range(4, 9):
        red_b[step]()
    red_a[8]()
    for block in range(16):
        for half in range(2):
            value = full[block // 8, half, block % 8 // 4, block % 4].reshape(256, 128)
            if block < 9:
                gsp_ref[block, :, 128 * half : 128 * half + 128] = value
            elif block < 12:
                gt_ref[block - 9, :, 128 * half : 128 * half + 128] = value
            else:
                gd_ref[block - 12, :, 128 * half : 128 * half + 128] = value


def solution(mesh):
    n_tm, n_grp = mesh.shape["tm"], mesh.shape["grp"]

    def body(frames_in, span_frames, w_spatial, w_temporal, w_down, cotangent):
        hbm = pl.BlockSpec(memory_space=pl.ANY)
        vmem = pl.BlockSpec(memory_space=pltpu.VMEM)
        scratch = [
            pltpu.VMEM((16, 128, 256), BF),
            pltpu.VMEM((16, 32, 256), BF),
            pltpu.VMEM((2304, 256), BF),
            pltpu.VMEM((768, 256), BF),
            pltpu.VMEM((1024, 256), BF),
            pltpu.VMEM((256, 256), BF),
            pltpu.VMEM((8, 64, 256), BF),
            pltpu.VMEM((10, 64, 256), BF),
            pltpu.VMEM((20, 4, 2, 16, 256), BF),
            pltpu.VMEM((16, 128, 256), BF),
            pltpu.VMEM((18, 160, 256), BF),
            pltpu.VMEM((16, 128, 256), BF),
            pltpu.VMEM((18, 160, 256), BF),
            pltpu.VMEM((256, 2048), BF),
            pltpu.VMEM((2, 128, 256), BF),
            pltpu.VMEM((16, 16, 256), BF),
            pltpu.VMEM((8, 16, 256), BF),
            pltpu.VMEM((2, 128, 256), BF),
            pltpu.VMEM((2, 64, 256), BF),
            pltpu.VMEM((18, 16, 256), BF),
            pltpu.VMEM((10, 16, 256), BF),
            pltpu.VMEM((3, 2048, 256), BF),
            pltpu.VMEM((4, 8, 64, 256), BF),
            pltpu.VMEM((2, 2, 8, 256, 128), BF),
            pltpu.VMEM((2, 8, 256, 128), BF),
            pltpu.VMEM((2, 8, 256, 128), BF),
            pltpu.VMEM((2, 2, 3, 256, 128), BF),
            pltpu.VMEM((2, 2, 4, 64, 128), BF),
            pltpu.VMEM((2, 2, 3, 64, 128), BF),
            pltpu.VMEM((2, 8, 16, 128), BF),
            pltpu.VMEM((2, 7, 16, 128), BF),
            pltpu.VMEM((2, 2, 2, 4, 4, 4, 16, 128), BF),
            pltpu.SemaphoreType.DMA((5,)),
            pltpu.SemaphoreType.DMA((10,)),
            pltpu.SemaphoreType.DMA((10,)),
            pltpu.SemaphoreType.DMA((2, 40)),
            pltpu.SemaphoreType.DMA((2, 40)),
        ]
        down, gx, gsp, gt, gd = pl.pallas_call(
            functools.partial(kernel, n_tm, n_grp),
            out_shape=(
                jax.ShapeDtypeStruct((16, 32, 256), BF),
                jax.ShapeDtypeStruct((16, 128, 256), BF),
                jax.ShapeDtypeStruct((9, 256, 256), BF),
                jax.ShapeDtypeStruct((3, 256, 256), BF),
                jax.ShapeDtypeStruct((4, 256, 256), BF),
            ),
            in_specs=[pl.BlockSpec(memory_space=pltpu.SMEM)] + [hbm] * 5,
            out_specs=(vmem,) * 5,
            scratch_shapes=scratch,
            compiler_params=pltpu.CompilerParams(
                collective_id=0, has_side_effects=True, vmem_limit_bytes=52 * 1024 * 1024
            ),
        )(
            span_frames,
            frames_in.reshape(16, 128, 256),
            cotangent.reshape(16, 32, 256),
            w_spatial.reshape(2304, 256),
            w_temporal.reshape(768, 256),
            w_down.reshape(1024, 256),
        )
        return (
            down.reshape(16, 8, 4, 256),
            gx.reshape(16, 16, 8, 256),
            gsp.astype(F32).reshape(3, 3, 256, 256),
            gt.astype(F32),
            gd.astype(F32).reshape(2, 2, 256, 256),
        )

    return jax.shard_map(
        body,
        mesh=mesh,
        in_specs=(P("tm", "grp", None, None), P("tm"), P(), P(), P(), P("tm", "grp", None, None)),
        out_specs=(P("tm", "grp", None, None), P("tm", "grp", None, None), P(), P(), P()),
        check_vma=False,
    )
```

time: 450 us -> 84.9 us (0.19)
  waiting for transfers between devices: 321 us -> 0 us
  Pallas kernels: 0 us -> 74.8 us
  matrix products: 30.7 us -> 0 us
  starting transfers between devices: 27.6 us -> 0 us
  local copies, waits for them, and re-layouts: 29.6 us -> 3.75 us
  blocking collectives: 17.8 us -> 0 us
  between operations: 15.2 us -> 1.3 us
    psum x1 -> x0, waiting for transfers between devices: 267 us -> none  [body(): lax.psum((grad_spatial, grad_temporal, grad_down), ('tm', 'grp'))]
    pallas_call x0 -> x1, Pallas kernels: none -> 74.8 us  [body(): pl.pallas_call(functools.partial(kernel, n_tm, n_grp), out_shape=(jax.Sha...]
    all_to_all x3 -> x0, waiting for transfers between devices: 50.9 us -> none  [the longest x1 24.8 us: body(): lax.all_to_all(grad_a_frames, 'grp', split_axis=1, concat_axis=0, tiled=T...]
    dot_general x39 -> x0, matrix products: 30.7 us -> none  [the longest x9 7.07 us: spatial_grad(): jnp.einsum('fhwc,fhwd->cd', piece, grads, preferred_element_type=jnp.floa...]
    all_to_all x1 -> x0, blocking collectives: 17.8 us -> none  [body(): lax.all_to_all(grad_s, 'grp', split_axis=0, concat_axis=1, tiled=True)]
    ppermute x2 -> x0, starting transfers between devices: 14.4 us -> none  [passed_along(): return lax.ppermute(value, axis, pairs)]
    all_to_all x3 -> x0, starting transfers between devices: 13.1 us -> none  [the longest x1 4.66 us: body(): lax.all_to_all(grad_a_frames, 'grp', split_axis=1, concat_axis=0, tiled=T...]
    unnamed x46 -> x5, local copies, waits for them, and re-layouts: 9.73 us -> 1.96 us
  transfers between devices with their start and end apart: 6 -> 0, of which waited for: 6 -> 0; matrix products, arithmetic and copies ran while one was open for 2% -> 0% of each run, Pallas kernels for 0% -> 0%
where the time goes in v1:
time: 84.9 us; the launch traced here: 84.7 us
  Pallas kernels  74.8 us (88%)
  other arithmetic  4.9 us (6%)
  local copies, waits for them, and re-layouts  3.75 us (4%)
  between operations  1.3 us (2%)
    pallas_call x1, Pallas kernels, body(): pl.pallas_call(functools.partial(kernel, n_tm, n_grp), out_shape=(jax.Sha...  74.8 us
    reshape x1, other arithmetic, body(): gsp.astype(F32).reshape(3, 3, 256, 256)  2.9 us
    unnamed x5, local copies, waits for them, and re-layouts  1.96 us

profile of v1, /device:TPU:1, one launch (start us, length us, event | category | flops | bytes accessed | tf_op | source)
XLA Modules:
  0.0 84.7 jit_solution(4105214230072354024)
XLA Ops:
  1.3 1.0 %reshape.44.cot_hbm = bf16[16,32,256]{2,1,0:T(8,128)(2,1)S(1)} reshape(bf16[16,8,4,256]{3,2,1,0:T(4,128)(2,1)} %param.11) | data formatting | bytes 524288 | tf_op jit(solution)/shard_map/reshape | solution.py:554
  2.3 0.0 copy-start
  2.3 1.0 %copy-done = bf16[3,256,256]{2,1,0:T(8,128)(2,1)S(1)} copy-done((bf16[3,256,256]{2,1,0:T(8,128)(2,1)S(1)}, bf16[3,256,256]{2,1,0:T(8,128)(2,1)}, u32[]{:S(2)}) %copy-start) | copy-done | bytes 393240
  3.3 74.8 %shard_map.101 = (bf16[16,32,256]{2,1,0:T(8,128)(2,1)S(1)}, bf16[16,128,256]{2,1,0:T(8,128)(2,1)}, bf16[9,256,256]{2,1,0:T(8,128)(2,1)}, bf16[3,256,256]{2,1,0:T(8,128)(2,1)S(1)}, bf16[4,256,256]{2,1,0:T(8,128)(2,1)S(1)}) custom-call(s32[1]{0:T(128)S(6)} %copy.12.span, bf16[16,128,256]{2,1,0:T(8,128)(2,1)} %bitcast.13, ...), custom_call_target="tpu_custom_call" | custom-call | tf_op jit(solution)/shard_map/pallas_call | solution.py:536
  78.1 0.8 reshape.48
  78.8 2.9 %convert.2 = f32[3,3,256,256]{3,2,1,0:T(8,128)} convert(bf16[3,3,256,256]{3,2,1,0:T(8,128)(2,1)} %bitcast.11) | non-fusion elementwise | flops 589824 | bytes 3538944 | tf_op jit(solution)/shard_map/reshape | solution.py:562
  81.7 0.0 copy-start.1
  81.7 0.9 %convert_element_type.2 = f32[3,256,256]{2,1,0:T(8,128)} convert(bf16[3,256,256]{2,1,0:T(8,128)(2,1)S(1)} %get-tuple-element.13) | non-fusion elementwise | flops 196608 | bytes 1179648 | tf_op jit(solution)/shard_map/convert_element_type | solution.py:563
  82.7 1.1 %convert.3 = f32[2,2,256,256]{3,2,1,0:T(8,128)} convert(bf16[2,2,256,256]{3,2,1,0:T(8,128)(2,1)S(1)} %bitcast.9) | non-fusion elementwise | flops 262144 | bytes 1572864 | tf_op jit(solution)/shard_map/reshape | solution.py:564
  83.7 0.0 copy-done.1
  83.7 1.0 %copy.13 = bf16[16,16,8,256]{3,2,1,0:T(8,128)(2,1)} copy(bf16[16,16,8,256]{3,2,1,0:T(8,128)(2,1)S(1)} %bitcast.14) | data formatting | bytes 2097152
Async XLA Ops:
  2.3 1.0 %copy-start = (bf16[3,256,256]{2,1,0:T(8,128)(2,1)S(1)}, bf16[3,256,256]{2,1,0:T(8,128)(2,1)}, u32[]{:S(2)}) copy-start(bf16[3,256,256]{2,1,0:T(8,128)(2,1)} %param.9) | copy-start | bytes 1179652
  81.7 2.0 %copy-start.1 = (bf16[16,128,256]{2,1,0:T(8,128)(2,1)S(1)}, bf16[16,128,256]{2,1,0:T(8,128)(2,1)}, u32[]{:S(2)}) copy-start(bf16[16,128,256]{2,1,0:T(8,128)(2,1)} %get-tuple-element.11) | copy-start | bytes 3145732

commit v2 on v1

v2 whole, which is shorter than its diff:
```python
import functools

import jax
import jax.numpy as jnp
from jax import lax
from jax.experimental import pallas as pl
from jax.experimental.pallas import tpu as pltpu
from jax.sharding import PartitionSpec as P

MESH = pl.DeviceIdType.MESH
BF = jnp.bfloat16
F32 = jnp.float32
NT = (((1,), (1,)), ((), ()))
TN = (((0,), (0,)), ((), ()))


def mm(a, b):
    return jnp.dot(a, b, preferred_element_type=F32)


def mm_nt(a, b):
    return lax.dot_general(a, b, NT, preferred_element_type=F32)


def mm_tn(a, b):
    return lax.dot_general(a, b, TN, preferred_element_type=F32)


def onehot(cond):
    return jnp.where(cond, 1.0, 0.0).astype(BF)


def iotas(rows, cols):
    shape = (rows, cols)
    return lax.broadcasted_iota(jnp.int32, shape, 0), lax.broadcasted_iota(jnp.int32, shape, 1)


def kernel(
    n_tm,
    n_grp,
    span,
    x_hbm,
    x_rows,
    cot_hbm,
    wsp_hbm,
    wt_hbm,
    wd_hbm,
    down_v,
    gx_v,
    full,
    xv,
    cv,
    wsp,
    wt,
    wd,
    perm,
    cown,
    cext,
    gy,
    gyo,
    gyo_t,
    cown_t,
    gs,
    xt,
    acts,
    acts_t,
    s_edge,
    s_corner,
    r_x,
    r_edge,
    r_corner,
    r_cot,
    r_next,
    r_ncorner,
    sp,
    y4,
    part,
    r_core,
    sum1,
    r_one,
    sum2,
    r_two,
    in_sem,
    h_send,
    h_recv,
    a_send,
    a_recv,
):
    t = lax.axis_index("tm")
    g = lax.axis_index("grp")
    core = lax.rem(t, 2)
    x = lax.rem(lax.div(t, 2), 2) * 2 + lax.rem(g, 2)
    y = lax.div(g, 2)
    z = lax.div(t, 4)
    count = span[0]

    def device(px, py, pz, pc):
        return (pz * 4 + lax.div(px, 2) * 2 + pc, py * 2 + lax.rem(px, 2))

    line = x * (1 - core) + y * core
    cross = y * (1 - core) + x * core

    def line_peer(d):
        px, py = lax.rem(x + d * (1 - core), 4), lax.rem(y + d * core, 4)
        return lax.rem(line + d, 4), device(px, py, z, core)

    def plane_peer(d, dz):
        px, py = lax.rem(x + d * core, 4), lax.rem(y + d * (1 - core), 4)
        pz = lax.rem(z + dz, 8)
        return lax.rem(cross + d, 4) * 8 + pz, device(px, py, pz, core)

    plane = [(d, dz) for d in (2, 1, 3, 0) for dz in (4, 3, 5, 2, 6, 1, 7, 0) if d + dz]
    mine = cross * 8 + z

    sibling = device(x, y, z, 1 - core)
    t_next, t_prev = lax.rem(t + 1, n_tm), lax.rem(t + n_tm - 1, n_tm)
    g_next, g_prev = lax.rem(g + 1, n_grp), lax.rem(g + n_grp - 1, n_grp)

    loads = [
        pltpu.make_async_copy(src, dst, in_sem.at[i])
        for i, (src, dst) in enumerate(
            ((cot_hbm, cv), (x_hbm, xv), (wd_hbm, wd), (wt_hbm, wt), (wsp_hbm, wsp))
        )
    ]
    for load in loads:
        load.start()

    partners = [(t, g_next), (t, g_prev), (t_next, g), (t_prev, g)]
    partners += [(t_next, g_next), (t_next, g_prev), (t_prev, g_next), (t_prev, g_prev)]
    partners += [sibling]
    partners += [line_peer(d)[1] for d in (1, 2, 3)]
    partners += [plane_peer(d, dz)[1] for d, dz in plane]
    barrier = pltpu.get_barrier_semaphore()
    for partner in partners:
        pl.semaphore_signal(barrier, inc=1, device_id=partner, device_id_type=MESH)

    r, q = iotas(256, 256)
    perm[...] = onehot((lax.rem(r, 16) == lax.div(q, 16)) & (lax.div(r, 16) == lax.rem(q, 16)))
    slot = lax.rem(lax.broadcasted_iota(jnp.int32, (256, 256), 0), 16)
    valid = slot < count

    zeros16 = jnp.zeros((18, 16, 256), BF)
    r_x[:, 13:16] = jnp.zeros((2, 3, 8, 256), BF)
    r_cot[:, 13:16] = jnp.zeros((2, 3, 4, 256), BF)
    for buffer in (acts, gs):
        buffer[:, 0:16, :] = zeros16
        buffer[:, 144:160, :] = zeros16

    def halo(index, src, dst, to):
        return pltpu.make_async_remote_copy(
            src_ref=src,
            dst_ref=dst,
            send_sem=h_send.at[index],
            recv_sem=h_recv.at[index],
            device_id=to,
            device_id_type=MESH,
        )

    used, first = pl.ds(0, 13), cot_hbm.at[pl.ds(0, 2)]
    cot_halos = [
        halo(0, cot_hbm.at[used, 7], r_cot.at[0, used], (t, g_next)),
        halo(1, cot_hbm.at[used, 0], r_cot.at[1, used], (t, g_prev)),
        halo(2, first, r_next, (t_prev, g)),
        halo(3, first.at[:, 7], r_ncorner.at[0], (t_prev, g_next)),
        halo(4, first.at[:, 0], r_ncorner.at[1], (t_prev, g_prev)),
    ]
    act_halos = [
        halo(5, x_rows.at[used, 15], r_x.at[0, used], (t, g_next)),
        halo(6, x_rows.at[used, 0], r_x.at[1, used], (t, g_prev)),
    ]
    edge_halos = [
        halo(7, s_edge, r_edge, (t_next, g)),
        halo(8, s_corner.at[0], r_corner.at[0], (t_next, g_next)),
        halo(9, s_corner.at[1], r_corner.at[1], (t_next, g_prev)),
    ]
    pl.semaphore_wait(barrier, len(partners))
    for copy in cot_halos + act_halos:
        copy.start()
    loads[1].wait()
    last = pl.ds(jnp.clip(count - 2, 0, 14), 2)
    s_edge[...] = xv[last]
    s_corner[0] = xv[last, 120:128, :].reshape(16, 256)
    s_corner[1] = xv[last, 0:8, :].reshape(16, 256)
    for copy in edge_halos:
        copy.start()

    def act(v):
        u = v * lax.rsqrt(jnp.mean(v * v, axis=-1, keepdims=True) + 1e-06)
        return u / (1.0 + jnp.exp(-u))

    r, q = iotas(256, 256)
    eye = onehot(r == q)
    for pair in range(8):
        v = mm(perm[...], xv[:, 16 * pair : 16 * pair + 16, :].reshape(256, 256))
        xt[2 * pair : 2 * pair + 2] = v.astype(BF).reshape(2, 128, 256)
        a = jnp.where(valid, act(v), 0.0).astype(BF)
        acts[2 * pair + 1 : 2 * pair + 3, 16:144, :] = a.reshape(2, 128, 256)
        acts_t[:, 256 * pair : 256 * pair + 256] = mm_nt(eye, a).astype(BF)

    loads[0].wait()
    for b in range(2):
        block = mm(perm[...], cv[:, 4 * b : 4 * b + 4].reshape(256, 256))
        cown[4 * b : 4 * b + 4] = jnp.where(valid, block, 0.0).astype(BF).reshape(4, 64, 256)

    loads[2].wait()
    for i in range(2):
        for j in range(2):
            tap = wd[pl.ds((2 * i + j) * 256, 256), :]
            piece = mm_nt(cown[...].reshape(512, 256), tap).astype(BF).reshape(8, 4, 16, 256)
            for row in range(8):
                gyo[2 * row + i, :, j] = piece[row]
    for k in range(8):
        now = gyo[2 * k : 2 * k + 2].reshape(256, 256)
        gyo_t[:, 256 * k : 256 * k + 256] = mm_nt(eye, now).astype(BF)
    for k in range(2):
        now = cown[4 * k : 4 * k + 4].reshape(256, 256)
        cown_t[:, 256 * k : 256 * k + 256] = mm_nt(eye, now).astype(BF)

    for copy in cot_halos:
        copy.wait()
    r, q = iotas(256, 32)
    put_next = onehot(
        (lax.div(r, 16) == lax.rem(q, 16))
        & (lax.rem(r, 16) == count + lax.div(q, 16))
        & (t < n_tm - 1)
    )
    for b in range(2):
        block = cown[4 * b : 4 * b + 4].reshape(256, 256).astype(F32)
        block += mm(put_next, r_next[:, 4 * b : 4 * b + 4].reshape(32, 256))
        cext[4 * b + 1 : 4 * b + 5] = block.astype(BF).reshape(4, 64, 256)
    r, q = iotas(64, 64)
    turn = onehot((lax.rem(r, 16) == lax.div(q, 4)) & (lax.div(r, 16) == lax.rem(q, 4)))
    r, q = iotas(64, 8)
    put_corner = onehot(
        (lax.div(r, 16) == lax.rem(q, 4))
        & (lax.rem(r, 16) == count + lax.div(q, 4))
        & (t < n_tm - 1)
    )
    for side, row, inside in ((0, 0, g > 0), (1, 9, g < n_grp - 1)):
        block = jnp.where(valid[:64], mm(turn, r_cot[side].reshape(64, 256)), 0.0)
        block += mm(put_corner, r_ncorner[side].reshape(8, 256))
        cext[row] = jnp.where(inside, block, 0.0).astype(BF)
    for i in range(2):
        for j in range(2):
            piece = mm_nt(cext[...].reshape(640, 256), wd[pl.ds((2 * i + j) * 256, 256), :])
            piece = piece.astype(BF).reshape(10, 4, 16, 256)
            for row in range(10):
                gy[2 * row + i, :, j] = piece[row]

    loads[3].wait()
    r, q = iotas(256, 256)
    same = lax.div(r, 16) == lax.div(q, 16)
    r, q = lax.rem(r, 16), lax.rem(q, 16)
    up1, up2 = onehot(same & (q == r + 1)), onehot(same & (q == r + 2))
    wt_back = jnp.concatenate([wt[512:768], wt[256:512], wt[0:256]], axis=1)

    for k in range(9):
        now = gy[2 * k + 1 : 2 * k + 3].reshape(256, 256)
        ext = jnp.concatenate([now, mm(up1, now).astype(BF), mm(up2, now).astype(BF)], axis=1)
        res = jnp.where(valid, mm_nt(ext, wt_back), 0.0).astype(BF)
        gs[2 * k : 2 * k + 2, 16:144, :] = res.reshape(2, 128, 256)

    def keep(block, value):
        value = value.astype(BF)
        n, k, a = block // 8, block % 8 // 4, block % 4
        part[n, k, a, 0:256] = value[:, :128]
        part[n, k, a, 256:512] = value[:, 128:]

    def reduction(n):
        def copy(index, src, dst, to):
            return pltpu.make_async_remote_copy(
                src_ref=src,
                dst_ref=dst,
                send_sem=a_send.at[n, index],
                recv_sem=a_recv.at[n, index],
                device_id=to,
                device_id_type=MESH,
            )

        cores = [copy(a, part.at[n, 1 - core, a], r_core.at[n, a], sibling) for a in range(4)]
        state = {}

        def begin(copies):
            for c in copies:
                c.start()
            state["now"] = copies

        def finish():
            for c in state["now"]:
                c.wait()

        def ahead(a):
            cores[a].wait()
            total = part[n, core, a].astype(F32) + r_core[n, a].astype(F32)
            sum1[n, a] = total.astype(BF)
            d = lax.rem(a + 4 - line, 4)
            px, py = a * (1 - core) + x * core, y * (1 - core) + a * core

            @pl.when(d != 0)
            def _():
                to = device(px, py, z, core)
                copy(3 + d, sum1.at[n, a], r_one.at[n, d - 1], to).start()

        def s2():
            for d in (1, 2, 3):
                copy(3 + d, sum1.at[n, 0], r_one.at[n, d - 1], line_peer(d)[1]).wait()
            total = sum1[n, line].astype(F32)
            for d in range(3):
                total += r_one[n, d].astype(F32)
            sum2[n] = total.astype(BF).reshape(32, 16, 128)
            copies = []
            for i, (d, dz) in enumerate(plane):
                p, to = plane_peer(d, dz)
                copies.append(copy(7 + i, sum2.at[n, p], r_two.at[n, i], to))
            begin(copies)

        def s3():
            finish()
            total = sum2[n, mine].astype(F32)
            for i in range(31):
                total += r_two[n, i].astype(F32)
            full[n, core, line, mine] = total.astype(BF)
            piece = full.at[n, core, line, mine]
            begin([copy(38 + i, piece, piece, plane_peer(d, dz)[1]) for i, (d, dz) in enumerate(plane)])

        def s4():
            finish()
            piece = full.at[n, core, line]
            state["line"] = [copy(68 + d, piece, piece, line_peer(d)[1]) for d in (1, 3, 2)]
            for c in state["line"]:
                c.start()
            begin([copy(72, piece, piece, sibling)])

        def s5():
            for c, d in zip(state["line"], (1, 3, 2)):
                c.wait()
                piece = full.at[n, core, lax.rem(line + 4 - d, 4)]
                state["now"].append(copy(72 + d, piece, piece, sibling))
                state["now"][-1].start()

        return cores, ahead, [s2, s3, s4, s5, finish]

    cores_a, ahead_a, red_a = reduction(0)
    cores_b, ahead_b, red_b = reduction(1)

    def spatial_grad(tap):
        i, j = tap // 3, tap % 3
        piece = gs[2 - i : 18 - i, 16 * (2 - j) : 16 * (2 - j) + 128, :].reshape(2048, 256)
        keep(tap, mm(acts_t[...], piece))

    for a in range(4):
        spatial_grad(a)
        spatial_grad(4 + a)
        cores_a[a].start()
    spatial_grad(8)
    for a in range(4):
        ahead_a(a)

    for copy in act_halos:
        copy.wait()
    for copy in edge_halos:
        copy.wait()
    r, q = iotas(256, 32)
    put_edge = onehot(
        (lax.div(r, 16) == lax.rem(q, 16)) & (lax.rem(r, 16) == 14 + lax.div(q, 16)) & (t > 0)
    )
    edge_act = act(r_edge[...].reshape(256, 256).astype(F32)).astype(BF).reshape(2, 128, 256)
    for k in range(8):
        block = acts[2 * k + 1 : 2 * k + 3, 16:144, :].reshape(256, 256).astype(F32)
        block += mm(put_edge, edge_act[:, 16 * k : 16 * k + 16].reshape(32, 256))
        acts[2 * k + 1 : 2 * k + 3, 16:144, :] = block.astype(BF).reshape(2, 128, 256)
    r, q = iotas(128, 128)
    turn = onehot((lax.rem(r, 16) == lax.div(q, 8)) & (lax.div(r, 16) == lax.rem(q, 8)))
    r, q = iotas(128, 16)
    put_corner = onehot(
        (lax.div(r, 16) == lax.rem(q, 8)) & (lax.rem(r, 16) == 14 + lax.div(q, 8)) & (t > 0)
    )
    for side, row, inside in ((0, 0, g > 0), (1, 17, g < n_grp - 1)):
        block = jnp.where(valid[:128], act(mm(turn, r_x[side].reshape(128, 256))), 0.0)
        block += mm(put_corner, act(r_corner[side].astype(F32)).astype(BF))
        acts[row, 16:144, :] = jnp.where(inside, block, 0.0).astype(BF)

    loads[4].wait()
    r, q = iotas(256, 256)
    same = lax.div(r, 16) == lax.div(q, 16)
    r, q = lax.rem(r, 16), lax.rem(q, 16)
    back1 = onehot(same & (q == lax.rem(r + 15, 16)))
    back2 = onehot(same & (q == lax.rem(r + 14, 16)))

    def taps(buffer, start, flip):
        pieces = []
        for i in range(3):
            for j in range(3):
                a, b = (2 - i, 2 - j) if flip else (i, j)
                piece = buffer[pl.ds(start + a, 4), 16 * b : 16 * b + 128, :]
                pieces.append(piece.reshape(512, 256))
        return jnp.concatenate(pieces, axis=1)

    slot5 = lax.rem(lax.broadcasted_iota(jnp.int32, (512, 256), 0), 16)
    valid5 = slot5 < count
    for k in range(4):
        res = mm(taps(acts, 4 * k, False), wsp[...]).astype(BF)
        one = [mm(back1, res[h : h + 256]).astype(BF) for h in (0, 256)]
        two = [mm(back2, res[h : h + 256]).astype(BF) for h in (0, 256)]
        one, two = jnp.concatenate(one, axis=0), jnp.concatenate(two, axis=0)
        sp[0, 512 * k : 512 * k + 512] = two
        sp[1, 512 * k : 512 * k + 512] = one
        sp[2, 512 * k : 512 * k + 512] = res
        total = mm(jnp.concatenate([two, one, res], axis=1), wt[...])
        total += xt[4 * k : 4 * k + 4].reshape(512, 256).astype(F32)
        total = jnp.where(valid5, total, 0.0).astype(BF).reshape(2, 2, 4, 2, 16, 256)
        for i in range(2):
            for j in range(2):
                y4[2 * i + j, 2 * k : 2 * k + 2] = total[:, i, :, j].reshape(2, 64, 256)

    for k in range(4):
        if k:
            keep(8 + k, mm(gyo_t[...], sp[k - 1]).T)
        keep(12 + k, mm(cown_t[...], y4[k].reshape(512, 256)).T)
        cores_b[k].start()
    for k in range(4):
        ahead_b(k)
    red_a[0]()
    ext = jnp.concatenate([y4[k].reshape(512, 256) for k in range(4)], axis=1)
    res = mm(ext, wd[...]).astype(BF)
    for b in range(2):
        block = mm(perm[...], res[256 * b : 256 * b + 256]).astype(BF)
        down_v[:, 16 * b : 16 * b + 16, :] = block.reshape(16, 16, 256)

    wsp_back = jnp.concatenate([wsp[256 * k : 256 * k + 256] for k in range(9)], axis=1)

    def finish_rows(k):
        ga = mm_nt(taps(gs, 4 * k, True), wsp_back)
        v = xt[pl.ds(4 * k, 4)].reshape(512, 256).astype(F32)
        inv = lax.rsqrt(jnp.mean(v * v, axis=-1, keepdims=True) + 1e-06)
        u = v * inv
        s = 1.0 / (1.0 + jnp.exp(-u))
        gu = ga * (s * (1.0 + u * (1.0 - s)))
        gv = inv * (gu - u * jnp.mean(gu * u, axis=-1, keepdims=True))
        res = gv + gyo[pl.ds(4 * k, 4)].reshape(512, 256).astype(F32)
        res = jnp.where(valid5, res, 0.0).astype(BF)
        for half in range(2):
            block = mm(perm[...], res[256 * half : 256 * half + 256]).astype(BF)
            rows = pl.ds(pl.multiple_of(32 * k + 16 * half, 16), 16)
            gx_v[:, rows, :] = block.reshape(16, 16, 256)

    pl.loop(0, 1)(finish_rows)
    red_b[0]()
    pl.loop(1, 2)(finish_rows)
    red_a[1]()
    pl.loop(2, 3)(finish_rows)
    red_b[1]()
    pl.loop(3, 4)(finish_rows)
    for step in (2, 3, 4):
        red_a[step]()
        red_b[step]()


def results(down, gx, full, down_out, gx_out, gsp_out, gt_out, gd_out, wide, cells, sem):
    copies = [pltpu.make_async_copy(gx, gx_out, sem.at[16])]
    copies[0].start()
    for block in range(16):
        for half in range(2):
            part = full[block // 8, block % 8 // 4, block % 4, 16 * half : 16 * half + 16]
            wide[block, :, 128 * half : 128 * half + 128] = part.reshape(256, 128).astype(F32)
        out = gsp_out.at[block] if block < 9 else gt_out.at[block - 9] if block < 12 else gd_out.at[block - 12]
        copies.append(pltpu.make_async_copy(wide.at[block], out, sem.at[block]))
        copies[-1].start()
    cells[...] = down[...].reshape(16, 8, 4, 256)
    copies.append(pltpu.make_async_copy(cells, down_out, sem.at[17]))
    copies[-1].start()
    for copy in copies:
        copy.wait()


def solution(mesh):
    n_tm, n_grp = mesh.shape["tm"], mesh.shape["grp"]

    def body(frames_in, span_frames, w_spatial, w_temporal, w_down, cotangent):
        hbm = pl.BlockSpec(memory_space=pltpu.HBM)
        vmem = pl.BlockSpec(memory_space=pltpu.VMEM)
        scratch = [
            pltpu.VMEM((16, 128, 256), BF),
            pltpu.VMEM((16, 8, 4, 256), BF),
            pltpu.VMEM((2304, 256), BF),
            pltpu.VMEM((768, 256), BF),
            pltpu.VMEM((1024, 256), BF),
            pltpu.VMEM((256, 256), BF),
            pltpu.VMEM((8, 64, 256), BF),
            pltpu.VMEM((10, 64, 256), BF),
            pltpu.VMEM((20, 4, 2, 16, 256), BF),
            pltpu.VMEM((16, 4, 2, 16, 256), BF),
            pltpu.VMEM((256, 2048), BF),
            pltpu.VMEM((256, 512), BF),
            pltpu.VMEM((18, 160, 256), BF),
            pltpu.VMEM((16, 128, 256), BF),
            pltpu.VMEM((18, 160, 256), BF),
            pltpu.VMEM((256, 2048), BF),
            pltpu.VMEM((2, 128, 256), BF),
            pltpu.VMEM((2, 16, 256), BF),
            pltpu.VMEM((2, 16, 8, 256), BF),
            pltpu.VMEM((2, 128, 256), BF),
            pltpu.VMEM((2, 16, 256), BF),
            pltpu.VMEM((2, 16, 4, 256), BF),
            pltpu.VMEM((2, 8, 4, 256), BF),
            pltpu.VMEM((2, 2, 4, 256), BF),
            pltpu.VMEM((3, 2048, 256), BF),
            pltpu.VMEM((4, 8, 64, 256), BF),
            pltpu.VMEM((2, 2, 4, 512, 128), BF),
            pltpu.VMEM((2, 4, 512, 128), BF),
            pltpu.VMEM((2, 4, 512, 128), BF),
            pltpu.VMEM((2, 3, 512, 128), BF),
            pltpu.VMEM((2, 32, 16, 128), BF),
            pltpu.VMEM((2, 31, 16, 128), BF),
            pltpu.SemaphoreType.DMA((5,)),
            pltpu.SemaphoreType.DMA((10,)),
            pltpu.SemaphoreType.DMA((10,)),
            pltpu.SemaphoreType.DMA((2, 76)),
            pltpu.SemaphoreType.DMA((2, 76)),
        ]
        down, gx, full = pl.pallas_call(
            functools.partial(kernel, n_tm, n_grp),
            out_shape=(
                pltpu.VMEM((16, 32, 256), BF),
                pltpu.VMEM((16, 128, 256), BF),
                pltpu.VMEM((2, 2, 4, 32, 16, 128), BF),
            ),
            in_specs=[pl.BlockSpec(memory_space=pltpu.SMEM)] + [hbm] * 6,
            out_specs=(vmem,) * 3,
            scratch_shapes=scratch,
            compiler_params=pltpu.CompilerParams(
                collective_id=0, has_side_effects=True, vmem_limit_bytes=42 * 1024 * 1024
            ),
        )(
            span_frames,
            *(
                pltpu.with_memory_space_constraint(value, pltpu.HBM)
                for value in (
                    frames_in.reshape(16, 128, 256),
                    frames_in,
                    cotangent,
                    w_spatial.reshape(2304, 256),
                    w_temporal.reshape(768, 256),
                    w_down.reshape(1024, 256),
                )
            ),
        )
        down, gx, gsp, gt, gd = pl.pallas_call(
            results,
            out_shape=(
                jax.ShapeDtypeStruct((16, 8, 4, 256), BF),
                jax.ShapeDtypeStruct((16, 128, 256), BF),
                jax.ShapeDtypeStruct((9, 256, 256), F32),
                jax.ShapeDtypeStruct((3, 256, 256), F32),
                jax.ShapeDtypeStruct((4, 256, 256), F32),
            ),
            in_specs=[vmem] * 3,
            out_specs=(hbm,) * 5,
            scratch_shapes=[
                pltpu.VMEM((16, 256, 256), F32),
                pltpu.VMEM((16, 8, 4, 256), BF),
                pltpu.SemaphoreType.DMA((18,)),
            ],
            compiler_params=pltpu.CompilerParams(vmem_limit_bytes=24 * 1024 * 1024),
        )(down, gx, full)
        return (
            down,
            gx.reshape(16, 16, 8, 256),
            gsp.reshape(3, 3, 256, 256),
            gt,
            gd.reshape(2, 2, 256, 256),
        )

    return jax.shard_map(
        body,
        mesh=mesh,
        in_specs=(P("tm", "grp", None, None), P("tm"), P(), P(), P(), P("tm", "grp", None, None)),
        out_specs=(P("tm", "grp", None, None), P("tm", "grp", None, None), P(), P(), P()),
        check_vma=False,
    )
```

time: 84.9 us -> 70.4 us (0.83)
  Pallas kernels: 74.8 us -> 68.9 us
  other arithmetic: 4.9 us -> 0 us
  local copies, waits for them, and re-layouts: 3.75 us -> 0 us
    pallas_call x1 -> x2, Pallas kernels: 74.8 us -> 68.9 us  [the longest x1 66.4 us: body(): pl.pallas_call(functools.partial(kernel, n_tm, n_grp), out_shape=(pltpu.V...]
    reshape x2 -> x0, other arithmetic: 3.95 us -> none  [the longest x1 2.9 us: body(): gsp.astype(F32).reshape(3, 3, 256, 256)]
    unnamed x5 -> x0, local copies, waits for them, and re-layouts: 1.96 us -> none
    reshape x2 -> x0, local copies, waits for them, and re-layouts: 1.78 us -> none  [the longest x1 1.02 us: body(): cotangent.reshape(16, 32, 256)]
    convert_element_type x1 -> x0, other arithmetic: 0.95 us -> none  [body(): gt.astype(F32)]
where the time goes in v2:
time: 70.4 us
  Pallas kernels  68.9 us (98%)
  between operations  1.45 us (2%)
    pallas_call x1, Pallas kernels, body(): pl.pallas_call(functools.partial(kernel, n_tm, n_grp), out_shape=(pltpu.V...  66.4 us
    pallas_call x1, Pallas kernels, body(): pl.pallas_call(results, out_shape=(jax.ShapeDtypeStruct((16, 8, 4, 256),...  2.55 us

profile of v2, /device:TPU:1, one launch (start us, length us, event | category | flops | bytes accessed | tf_op | source)
XLA Modules:
  0.0 70.4 jit_solution(1553810089962937229)
XLA Ops:
  1.3 66.4 %shard_map.101 = (bf16[16,32,256]{2,1,0:T(8,128)(2,1)S(1)}, bf16[16,128,256]{2,1,0:T(8,128)(2,1)S(1)}, bf16[2,2,4,32,16,128]{5,4,3,2,1,0:T(8,128)(2,1)S(1)}) custom-call(s32[1]{0:T(128)S(6)} %copy.11.span, bf16[16,128,256]{2,1,0:T(8,128)(2,1)} %bitcast.7, bf16[16,16,8,256]{3,2,1,0:T(8,128)(2,1)} %x_rows.1, bf16[16,8,4,256]{3,2,1,0:T(4,128)(2,1)} %cot_hbm.1, ...), custom_call_target="tpu_custom_call" | custom-call | tf_op jit(solution)/shard_map/pallas_call | solution.py:521
  67.6 2.6 %shard_map.102 = (bf16[16,8,4,256]{3,2,1,0:T(4,128)(2,1)}, bf16[16,128,256]{2,1,0:T(8,128)(2,1)}, f32[9,256,256]{2,1,0:T(8,128)}, f32[3,256,256]{2,1,0:T(8,128)}, f32[4,256,256]{2,1,0:T(8,128)}) custom-call(bf16[16,32,256]{2,1,0:T(8,128)(2,1)S(1)} %get-tuple-element.13.down, bf16[16,128,256]{2,1,0:T(8,128)(2,1)S(1)} %get-tuple-element.14.gx, ...), custom_call_target="tpu_custom_call" | custom-call | tf_op jit(solution)/shard_map/pallas_call | solution.py:548

commit v3 on v2

--- a/solution.py
+++ b/solution.py
@@ -74,6 +74,8 @@
     r_ncorner,
     sp,
     y4,
+    grad_a,
+    grad_v,
     part,
     r_core,
     sum1,
@@ -263,8 +265,8 @@
     def keep(block, value):
         value = value.astype(BF)
         n, k, a = block // 8, block % 8 // 4, block % 4
-        part[n, k, a, 0:256] = value[:, :128]
-        part[n, k, a, 256:512] = value[:, 128:]
+        part[n, k, a, 0:16] = value[:, :128].reshape(16, 16, 128)
+        part[n, k, a, 16:32] = value[:, 128:].reshape(16, 16, 128)
 
     def reduction(n):
         def copy(index, src, dst, to):
@@ -289,30 +291,38 @@
             for c in state["now"]:
                 c.wait()
 
-        def ahead(a):
-            cores[a].wait()
-            total = part[n, core, a].astype(F32) + r_core[n, a].astype(F32)
-            sum1[n, a] = total.astype(BF)
-            d = lax.rem(a + 4 - line, 4)
-            px, py = a * (1 - core) + x * core, y * (1 - core) + a * core
-
-            @pl.when(d != 0)
-            def _():
-                to = device(px, py, z, core)
-                copy(3 + d, sum1.at[n, a], r_one.at[n, d - 1], to).start()
+        def chunk(e):
+            return pl.ds(8 * lax.rem(cross + e, 4), 8)
+
+        def line_copy(d, e):
+            a, to = line_peer(d)
+            index = 4 + 4 * (d - 1) + e
+            return copy(index, sum1.at[n, a, chunk(e)], r_one.at[n, d - 1, chunk(e)], to)
+
+        def s1():
+            for a in range(4):
+                cores[a].wait()
+                total = part[n, core, a].astype(F32) + r_core[n, a].astype(F32)
+                sum1[n, a] = total.astype(BF)
+            for e in (2, 1, 3, 0):
+                for d in (2, 1, 3):
+                    line_copy(d, e).start()
 
         def s2():
-            for d in (1, 2, 3):
-                copy(3 + d, sum1.at[n, 0], r_one.at[n, d - 1], line_peer(d)[1]).wait()
-            total = sum1[n, line].astype(F32)
-            for d in range(3):
-                total += r_one[n, d].astype(F32)
-            sum2[n] = total.astype(BF).reshape(32, 16, 128)
             copies = []
-            for i, (d, dz) in enumerate(plane):
-                p, to = plane_peer(d, dz)
-                copies.append(copy(7 + i, sum2.at[n, p], r_two.at[n, i], to))
-            begin(copies)
+            for e in (2, 1, 3, 0):
+                for d in (2, 1, 3):
+                    line_copy(d, e).wait()
+                total = sum1[n, line, chunk(e)].astype(F32)
+                for d in range(3):
+                    total += r_one[n, d, chunk(e)].astype(F32)
+                sum2[n, chunk(e)] = total.astype(BF)
+                for i, (d, dz) in enumerate(plane):
+                    if d == e:
+                        p, to = plane_peer(d, dz)
+                        copies.append(copy(16 + i, sum2.at[n, p], r_two.at[n, i], to))
+                        copies[-1].start()
+            state["now"] = copies
 
         def s3():
             finish()
@@ -321,24 +331,32 @@
                 total += r_two[n, i].astype(F32)
             full[n, core, line, mine] = total.astype(BF)
             piece = full.at[n, core, line, mine]
-            begin([copy(38 + i, piece, piece, plane_peer(d, dz)[1]) for i, (d, dz) in enumerate(plane)])
+            begin([copy(47 + i, piece, piece, plane_peer(d, dz)[1]) for i, (d, dz) in enumerate(plane)])
 
         def s4():
-            finish()
-            piece = full.at[n, core, line]
-            state["line"] = [copy(68 + d, piece, piece, line_peer(d)[1]) for d in (1, 3, 2)]
-            for c in state["line"]:
-                c.start()
-            begin([copy(72, piece, piece, sibling)])
+            state["line"], copies = {}, []
+            for e in (0, 1, 3, 2):
+                for c, (d, dz) in zip(state["now"], plane):
+                    if d == e:
+                        c.wait()
+                piece = full.at[n, core, line, chunk(4 - e)]
+                for d in (2, 1, 3):
+                    c = copy(78 + 4 * (d - 1) + e, piece, piece, line_peer(d)[1])
+                    c.start()
+                    state["line"][d, e] = c
+                copies.append(copy(90 + e, piece, piece, sibling))
+                copies[-1].start()
+            state["now"] = copies
 
         def s5():
-            for c, d in zip(state["line"], (1, 3, 2)):
-                c.wait()
-                piece = full.at[n, core, lax.rem(line + 4 - d, 4)]
-                state["now"].append(copy(72 + d, piece, piece, sibling))
-                state["now"][-1].start()
-
-        return cores, ahead, [s2, s3, s4, s5, finish]
+            for e in (0, 1, 3, 2):
+                for d in (1, 3, 2):
+                    state["line"][d, e].wait()
+                    piece = full.at[n, core, lax.rem(line + 4 - d, 4), chunk(4 - e)]
+                    state["now"].append(copy(94 + 4 * (d - 1) + e, piece, piece, sibling))
+                    state["now"][-1].start()
+
+        return cores, s1, [s2, s3, s4, s5, finish]
 
     cores_a, ahead_a, red_a = reduction(0)
     cores_b, ahead_b, red_b = reduction(1)
@@ -353,8 +371,7 @@
         spatial_grad(4 + a)
         cores_a[a].start()
     spatial_grad(8)
-    for a in range(4):
-        ahead_a(a)
+    ahead_a()
 
     for copy in act_halos:
         copy.wait()
@@ -392,34 +409,32 @@
         for i in range(3):
             for j in range(3):
                 a, b = (2 - i, 2 - j) if flip else (i, j)
-                piece = buffer[pl.ds(start + a, 4), 16 * b : 16 * b + 128, :]
-                pieces.append(piece.reshape(512, 256))
+                piece = buffer[start + a : start + a + 2, 16 * b : 16 * b + 128, :]
+                pieces.append(piece.reshape(256, 256))
         return jnp.concatenate(pieces, axis=1)
 
-    slot5 = lax.rem(lax.broadcasted_iota(jnp.int32, (512, 256), 0), 16)
-    valid5 = slot5 < count
-    for k in range(4):
-        res = mm(taps(acts, 4 * k, False), wsp[...]).astype(BF)
-        one = [mm(back1, res[h : h + 256]).astype(BF) for h in (0, 256)]
-        two = [mm(back2, res[h : h + 256]).astype(BF) for h in (0, 256)]
-        one, two = jnp.concatenate(one, axis=0), jnp.concatenate(two, axis=0)
-        sp[0, 512 * k : 512 * k + 512] = two
-        sp[1, 512 * k : 512 * k + 512] = one
-        sp[2, 512 * k : 512 * k + 512] = res
-        total = mm(jnp.concatenate([two, one, res], axis=1), wt[...])
-        total += xt[4 * k : 4 * k + 4].reshape(512, 256).astype(F32)
-        total = jnp.where(valid5, total, 0.0).astype(BF).reshape(2, 2, 4, 2, 16, 256)
+    for k in range(8):
+        sp[2, 256 * k : 256 * k + 256] = mm(taps(acts, 2 * k, False), wsp[...]).astype(BF)
+    for k in range(8):
+        rows = slice(256 * k, 256 * k + 256)
+        now = sp[2, rows]
+        sp[1, rows] = mm(back1, now).astype(BF)
+        sp[0, rows] = mm(back2, now).astype(BF)
+    for k in range(8):
+        rows = slice(256 * k, 256 * k + 256)
+        ext = jnp.concatenate([sp[0, rows], sp[1, rows], sp[2, rows]], axis=1)
+        total = mm(ext, wt[...]) + xt[2 * k : 2 * k + 2].reshape(256, 256).astype(F32)
+        total = jnp.where(valid, total, 0.0).astype(BF).reshape(2, 4, 2, 16, 256)
         for i in range(2):
             for j in range(2):
-                y4[2 * i + j, 2 * k : 2 * k + 2] = total[:, i, :, j].reshape(2, 64, 256)
+                y4[2 * i + j, k] = total[i, :, j].reshape(64, 256)
 
     for k in range(4):
         if k:
             keep(8 + k, mm(gyo_t[...], sp[k - 1]).T)
         keep(12 + k, mm(cown_t[...], y4[k].reshape(512, 256)).T)
         cores_b[k].start()
-    for k in range(4):
-        ahead_b(k)
+    ahead_b()
     red_a[0]()
     ext = jnp.concatenate([y4[k].reshape(512, 256) for k in range(4)], axis=1)
     res = mm(ext, wd[...]).astype(BF)
@@ -429,28 +444,35 @@
 
     wsp_back = jnp.concatenate([wsp[256 * k : 256 * k + 256] for k in range(9)], axis=1)
 
-    def finish_rows(k):
-        ga = mm_nt(taps(gs, 4 * k, True), wsp_back)
-        v = xt[pl.ds(4 * k, 4)].reshape(512, 256).astype(F32)
+    def grad_acts(k):
+        grad_a[256 * k : 256 * k + 256] = mm_nt(taps(gs, 2 * k, True), wsp_back)
+
+    def grad_rows(k):
+        ga = grad_a[256 * k : 256 * k + 256]
+        v = xt[2 * k : 2 * k + 2].reshape(256, 256).astype(F32)
         inv = lax.rsqrt(jnp.mean(v * v, axis=-1, keepdims=True) + 1e-06)
         u = v * inv
         s = 1.0 / (1.0 + jnp.exp(-u))
         gu = ga * (s * (1.0 + u * (1.0 - s)))
         gv = inv * (gu - u * jnp.mean(gu * u, axis=-1, keepdims=True))
-        res = gv + gyo[pl.ds(4 * k, 4)].reshape(512, 256).astype(F32)
-        res = jnp.where(valid5, res, 0.0).astype(BF)
-        for half in range(2):
-            block = mm(perm[...], res[256 * half : 256 * half + 256]).astype(BF)
-            rows = pl.ds(pl.multiple_of(32 * k + 16 * half, 16), 16)
-            gx_v[:, rows, :] = block.reshape(16, 16, 256)
-
-    pl.loop(0, 1)(finish_rows)
+        res = gv + gyo[2 * k : 2 * k + 2].reshape(256, 256).astype(F32)
+        grad_v[256 * k : 256 * k + 256] = jnp.where(valid, res, 0.0).astype(BF)
+
+    def turn_rows(k):
+        block = mm(perm[...], grad_v[256 * k : 256 * k + 256]).astype(BF)
+        gx_v[:, 16 * k : 16 * k + 16, :] = block.reshape(16, 16, 256)
+
+    for k in range(8):
+        grad_acts(k)
     red_b[0]()
-    pl.loop(1, 2)(finish_rows)
+    for k in range(4):
+        grad_rows(k)
     red_a[1]()
-    pl.loop(2, 3)(finish_rows)
+    for k in range(4, 8):
+        grad_rows(k)
     red_b[1]()
-    pl.loop(3, 4)(finish_rows)
+    for k in range(8):
+        turn_rows(k)
     for step in (2, 3, 4):
         red_a[step]()
         red_b[step]()
@@ -506,17 +528,19 @@
             pltpu.VMEM((2, 2, 4, 256), BF),
             pltpu.VMEM((3, 2048, 256), BF),
             pltpu.VMEM((4, 8, 64, 256), BF),
-            pltpu.VMEM((2, 2, 4, 512, 128), BF),
-            pltpu.VMEM((2, 4, 512, 128), BF),
-            pltpu.VMEM((2, 4, 512, 128), BF),
-            pltpu.VMEM((2, 3, 512, 128), BF),
+            pltpu.VMEM((2048, 256), F32),
+            pltpu.VMEM((2048, 256), BF),
+            pltpu.VMEM((2, 2, 4, 32, 16, 128), BF),
+            pltpu.VMEM((2, 4, 32, 16, 128), BF),
+            pltpu.VMEM((2, 4, 32, 16, 128), BF),
+            pltpu.VMEM((2, 3, 32, 16, 128), BF),
             pltpu.VMEM((2, 32, 16, 128), BF),
             pltpu.VMEM((2, 31, 16, 128), BF),
             pltpu.SemaphoreType.DMA((5,)),
             pltpu.SemaphoreType.DMA((10,)),
             pltpu.SemaphoreType.DMA((10,)),
-            pltpu.SemaphoreType.DMA((2, 76)),
-            pltpu.SemaphoreType.DMA((2, 76)),
+            pltpu.SemaphoreType.DMA((2, 106)),
+            pltpu.SemaphoreType.DMA((2, 106)),
         ]
         down, gx, full = pl.pallas_call(
             functools.partial(kernel, n_tm, n_grp),

time: 70.4 us -> 63.4 us (0.901)
  Pallas kernels: 68.9 us -> 61.9 us
    pallas_call x1, Pallas kernels: 66.4 us -> 59.4 us  [body(): pl.pallas_call(functools.partial(kernel, n_tm, n_grp), out_shape=(pltpu.V...]
where the time goes in v3:
time: 63.4 us
  Pallas kernels  61.9 us (98%)
  between operations  1.45 us (2%)
    pallas_call x1, Pallas kernels, body(): pl.pallas_call(functools.partial(kernel, n_tm, n_grp), out_shape=(pltpu.V...  59.4 us
    pallas_call x1, Pallas kernels, body(): pl.pallas_call(results, out_shape=(jax.ShapeDtypeStruct((16, 8, 4, 256),...  2.55 us

profile of v3, /device:TPU:1, one launch (start us, length us, event | category | flops | bytes accessed | tf_op | source)
XLA Modules:
  0.0 63.4 jit_solution(750243417527349274)
XLA Ops:
  1.3 59.4 %shard_map.101 = (bf16[16,32,256]{2,1,0:T(8,128)(2,1)S(1)}, bf16[16,128,256]{2,1,0:T(8,128)(2,1)S(1)}, bf16[2,2,4,32,16,128]{5,4,3,2,1,0:T(8,128)(2,1)S(1)}) custom-call(s32[1]{0:T(128)S(6)} %copy.11.span, bf16[16,128,256]{2,1,0:T(8,128)(2,1)} %bitcast.7, bf16[16,16,8,256]{3,2,1,0:T(8,128)(2,1)} %x_rows.1, bf16[16,8,4,256]{3,2,1,0:T(4,128)(2,1)} %cot_hbm.1, ...), custom_call_target="tpu_custom_call" | custom-call | tf_op jit(solution)/shard_map/pallas_call | solution.py:545
  60.6 2.6 %shard_map.102 = (bf16[16,8,4,256]{3,2,1,0:T(4,128)(2,1)}, bf16[16,128,256]{2,1,0:T(8,128)(2,1)}, f32[9,256,256]{2,1,0:T(8,128)}, f32[3,256,256]{2,1,0:T(8,128)}, f32[4,256,256]{2,1,0:T(8,128)}) custom-call(bf16[16,32,256]{2,1,0:T(8,128)(2,1)S(1)} %get-tuple-element.13.down, bf16[16,128,256]{2,1,0:T(8,128)(2,1)S(1)} %get-tuple-element.14.gx, ...), custom_call_target="tpu_custom_call" | custom-call | tf_op jit(solution)/shard_map/pallas_call | solution.py:572

commit v4 on v3

--- a/solution.py
+++ b/solution.py
@@ -176,14 +176,14 @@
         halo(9, s_corner.at[1], r_corner.at[1], (t_next, g_prev)),
     ]
     pl.semaphore_wait(barrier, len(partners))
-    for copy in cot_halos + act_halos:
+    for copy in cot_halos:
         copy.start()
     loads[1].wait()
     last = pl.ds(jnp.clip(count - 2, 0, 14), 2)
     s_edge[...] = xv[last]
     s_corner[0] = xv[last, 120:128, :].reshape(16, 256)
     s_corner[1] = xv[last, 0:8, :].reshape(16, 256)
-    for copy in edge_halos:
+    for copy in edge_halos + act_halos:
         copy.start()
 
     def act(v):

time: 63.4 us -> 63.5 us (level)
  no operation moved by 1% of the time
where the time goes in v4:
time: 63.5 us; the launch traced here: 63.4 us
  Pallas kernels  61.9 us (97%)
  between operations  1.45 us (2%)
    pallas_call x1, Pallas kernels, body(): pl.pallas_call(functools.partial(kernel, n_tm, n_grp), out_shape=(pltpu.V...  59.4 us
    pallas_call x1, Pallas kernels, body(): pl.pallas_call(results, out_shape=(jax.ShapeDtypeStruct((16, 8, 4, 256),...  2.55 us

profile of v4, /device:TPU:1, one launch (start us, length us, event | category | flops | bytes accessed | tf_op | source)
XLA Modules:
  0.0 63.4 jit_solution(13595026290517720371)
XLA Ops:
  1.3 59.4 %shard_map.101 = (bf16[16,32,256]{2,1,0:T(8,128)(2,1)S(1)}, bf16[16,128,256]{2,1,0:T(8,128)(2,1)S(1)}, bf16[2,2,4,32,16,128]{5,4,3,2,1,0:T(8,128)(2,1)S(1)}) custom-call(s32[1]{0:T(128)S(6)} %copy.11.span, bf16[16,128,256]{2,1,0:T(8,128)(2,1)} %bitcast.7, bf16[16,16,8,256]{3,2,1,0:T(8,128)(2,1)} %x_rows.1, bf16[16,8,4,256]{3,2,1,0:T(4,128)(2,1)} %cot_hbm.1, ...), custom_call_target="tpu_custom_call" | custom-call | tf_op jit(solution)/shard_map/pallas_call | solution.py:545
  60.6 2.6 %shard_map.102 = (bf16[16,8,4,256]{3,2,1,0:T(4,128)(2,1)}, bf16[16,128,256]{2,1,0:T(8,128)(2,1)}, f32[9,256,256]{2,1,0:T(8,128)}, f32[3,256,256]{2,1,0:T(8,128)}, f32[4,256,256]{2,1,0:T(8,128)}) custom-call(bf16[16,32,256]{2,1,0:T(8,128)(2,1)S(1)} %get-tuple-element.13.down, bf16[16,128,256]{2,1,0:T(8,128)(2,1)S(1)} %get-tuple-element.14.gx, ...), custom_call_target="tpu_custom_call" | custom-call | tf_op jit(solution)/shard_map/pallas_call | solution.py:572
